TPU v7x, 32 devices: a whole 2x2x4 slice. The times are simulated.
32 devices in a mesh: dp: 16 (over z, y, core), tensor: 2 (over x).
Axes of the slice: x: 2, y: 2, z: 4, core: 2. Of those that a mesh axis runs over, the one named last changes fastest.
Arguments:
- tokens: bfloat16 [1024, 32, 1024], P('tensor', 'dp'), may hold values from -6 to 6
- d_out: bfloat16 [1024, 32, 1024], P('tensor', 'dp'), may hold values from -6 to 6
- ln1_gain: bfloat16 [1024], P('dp'), may hold values from 0.099609375 to 1.8984375
- ln1_bias: bfloat16 [1024], P('dp'), may hold values from -1.75 to 1.75
- w_qkv: bfloat16 [3, 1024, 1024], P(None, 'dp', 'tensor'), may hold values from -0.1875 to 0.1875
- w_out: bfloat16 [1024, 1024], P('tensor', 'dp'), may hold values from -3 to 3
- ln2_gain: bfloat16 [1024], P('dp'), may hold values from 0.099609375 to 1.8984375
- ln2_bias: bfloat16 [1024], P('dp'), may hold values from -1.75 to 1.75
- w_up: bfloat16 [1024, 4096], P('dp', 'tensor'), may hold values from -0.1875 to 0.1875
- w_down: bfloat16 [4096, 1024], P('tensor', 'dp'), may hold values from -0.09375 to 0.09375
Outputs:
- block_out: bfloat16 [1024, 32, 1024], P('tensor', 'dp')
- input_grad: bfloat16 [1024, 32, 1024], P('tensor', 'dp')
- grad_ln1_gain: float32 [1024], P('dp')
- grad_ln1_bias: float32 [1024], P('dp')
- grad_w_qkv: float32 [3, 1024, 1024], P(None, 'dp', 'tensor')
- grad_w_out: float32 [1024, 1024], P('tensor', 'dp')
- grad_ln2_gain: float32 [1024], P('dp')
- grad_ln2_bias: float32 [1024], P('dp')
- grad_w_up: float32 [1024, 4096], P('dp', 'tensor')
- grad_w_down: float32 [4096, 1024], P('tensor', 'dp')
All inputs are finite; a program needn't handle non-finite values.
Results may differ from a plain program's by a relative error of at most 0.023.
Values may be sent and summed in bfloat16 or wider, within the bound.
No kernel may reach another device: no remote copies, remote signals or barrier semaphores. Data moves between devices by JAX's collectives and lax.ppermute only.
A program may use at most 256 MiB of HBM per device.

v0:
```python
import jax
import jax.numpy as jnp
from jax import lax
from jax.sharding import PartitionSpec as P

HEAD_DIM = 64
EPSILON = 1e-05


def norm_rows(values, norm_gain, norm_bias):
    center = jnp.mean(values, axis=-1, keepdims=True)
    centered = values - center
    inverse = lax.rsqrt(jnp.mean(centered * centered, axis=-1, keepdims=True) + EPSILON)
    normal = centered * inverse
    return (normal * norm_gain + norm_bias, normal, inverse)


def norm_back(grad_in, normal, inverse, norm_gain):
    gain_grad = jnp.sum(grad_in * normal, axis=(0, 1))
    bias_grad = jnp.sum(grad_in, axis=(0, 1))
    scaled = grad_in * norm_gain
    first = jnp.mean(scaled, axis=-1, keepdims=True)
    second = jnp.mean(scaled * normal, axis=-1, keepdims=True)
    return (inverse * (scaled - first - normal * second), gain_grad, bias_grad)


def causal_mask(length):
    row_index = lax.broadcasted_iota(jnp.int32, (length, length), 0)
    column_index = lax.broadcasted_iota(jnp.int32, (length, length), 1)
    return column_index <= row_index


def attend_forward(triple):
    queries, key_rows, value_rows = triple
    scores = jnp.einsum(
        "qhd,khd->hqk", queries, key_rows, preferred_element_type=jnp.float32
    ) * HEAD_DIM ** (-0.5)
    scores = jnp.where(causal_mask(queries.shape[0]), scores, -1e30)
    row_max = jnp.max(scores, axis=-1, keepdims=True)
    weights = jnp.exp(scores - row_max)
    totals = jnp.sum(weights, axis=-1, keepdims=True)
    shares = (weights / totals).astype(jnp.bfloat16)
    mixed = jnp.einsum("hqk,khd->qhd", shares, value_rows, preferred_element_type=jnp.float32)
    return (mixed.astype(jnp.bfloat16), row_max + jnp.log(totals))


def attend_back(group):
    queries, key_rows, value_rows, grad_mixed, log_total = group
    factor = HEAD_DIM ** (-0.5)
    scores = (
        jnp.einsum("qhd,khd->hqk", queries, key_rows, preferred_element_type=jnp.float32) * factor
    )
    scores = jnp.where(causal_mask(queries.shape[0]), scores, -1e30)
    shares = jnp.exp(scores - log_total)
    grad_value = jnp.einsum(
        "hqk,qhd->khd", shares.astype(jnp.bfloat16), grad_mixed, preferred_element_type=jnp.float32
    )
    grad_shares = jnp.einsum(
        "qhd,khd->hqk", grad_mixed, value_rows, preferred_element_type=jnp.float32
    )
    inner = jnp.sum(shares * grad_shares, axis=-1, keepdims=True)
    grad_scores = (shares * (grad_shares - inner)).astype(jnp.bfloat16)
    grad_query = (
        jnp.einsum("hqk,khd->qhd", grad_scores, key_rows, preferred_element_type=jnp.float32)
        * factor
    )
    grad_key = (
        jnp.einsum("hqk,qhd->khd", grad_scores, queries, preferred_element_type=jnp.float32)
        * factor
    )
    return jnp.stack([grad_query, grad_key, grad_value]).astype(jnp.bfloat16)


def on_device(tokens, d_out, ln1_gain, ln1_bias, w_qkv, w_out, ln2_gain, ln2_bias, w_up, w_down):
    local_rows, seq_count, width = tokens.shape
    gathered = (
        lax.all_gather(ln1_gain, "dp", axis=0, tiled=True),
        lax.all_gather(ln1_bias, "dp", axis=0, tiled=True),
        lax.all_gather(w_qkv, "dp", axis=1, tiled=True),
        lax.all_gather(w_out, "dp", axis=1, tiled=True),
        lax.all_gather(ln2_gain, "dp", axis=0, tiled=True),
        lax.all_gather(ln2_bias, "dp", axis=0, tiled=True),
        lax.all_gather(w_up, "dp", axis=0, tiled=True),
        lax.all_gather(w_down, "dp", axis=1, tiled=True),
    )
    gain_one, bias_one, qkv_weight, out_weight, gain_two, bias_two, up_weight, down_weight = (
        gathered
    )
    residual = tokens.astype(jnp.float32)
    normed_one, normal_one, inverse_one = norm_rows(
        residual, gain_one.astype(jnp.float32), bias_one.astype(jnp.float32)
    )
    low_one = normed_one.astype(jnp.bfloat16)
    rows_one = lax.all_gather(low_one, "tensor", axis=0, tiled=True)
    full_rows = rows_one.shape[0]
    projected = jnp.einsum(
        "tgd,cde->cgte", rows_one, qkv_weight, preferred_element_type=jnp.float32
    ).astype(jnp.bfloat16)
    local_width = projected.shape[3]
    heads_local = local_width // HEAD_DIM
    split_heads = projected.reshape(3, seq_count, full_rows, heads_local, HEAD_DIM)
    mixed, log_total = lax.map(attend_forward, (split_heads[0], split_heads[1], split_heads[2]))
    mixed = mixed.reshape(seq_count, full_rows, local_width)
    piece_rows = mixed
    hidden = residual + lax.psum_scatter(
        jnp.einsum(
            "gte,ed->tgd", piece_rows, out_weight, preferred_element_type=jnp.float32
        ).astype(jnp.bfloat16),
        "tensor",
        scatter_dimension=0,
        tiled=True,
    ).astype(jnp.float32)
    normed_two, normal_two, inverse_two = norm_rows(
        hidden, gain_two.astype(jnp.float32), bias_two.astype(jnp.float32)
    )
    low_two = normed_two.astype(jnp.bfloat16)
    rows_two = lax.all_gather(low_two, "tensor", axis=0, tiled=True)
    upward = jnp.einsum("tgd,df->tgf", rows_two, up_weight, preferred_element_type=jnp.float32)
    active = jax.nn.gelu(upward, approximate=True).astype(jnp.bfloat16)
    piece_rows = active
    block_sum = lax.psum_scatter(
        jnp.einsum(
            "tgf,fd->tgd", piece_rows, down_weight, preferred_element_type=jnp.float32
        ).astype(jnp.bfloat16),
        "tensor",
        scatter_dimension=0,
        tiled=True,
    ).astype(jnp.float32)
    block_out = (hidden + block_sum).astype(jnp.bfloat16)
    grad_rows = lax.all_gather(d_out, "tensor", axis=0, tiled=True)
    grad_down = jnp.einsum("tgf,tgd->fd", active, grad_rows, preferred_element_type=jnp.float32)
    grad_active = jnp.einsum(
        "tgd,fd->tgf", grad_rows, down_weight, preferred_element_type=jnp.float32
    )
    gelu_pull = jax.vjp(lambda inner: jax.nn.gelu(inner, approximate=True), upward)[1]
    grad_upward = gelu_pull(grad_active)[0].astype(jnp.bfloat16)
    grad_up = jnp.einsum("tgd,tgf->df", rows_two, grad_upward, preferred_element_type=jnp.float32)
    piece_rows = grad_upward
    grad_normed_two = lax.psum_scatter(
        jnp.einsum("tgf,df->tgd", piece_rows, up_weight, preferred_element_type=jnp.float32).astype(
            jnp.bfloat16
        ),
        "tensor",
        scatter_dimension=0,
        tiled=True,
    ).astype(jnp.float32)
    grad_hidden_norm, gain_two_grad, bias_two_grad = norm_back(
        grad_normed_two, normal_two, inverse_two, gain_two.astype(jnp.float32)
    )
    grad_hidden = d_out.astype(jnp.float32) + grad_hidden_norm
    low_hidden = grad_hidden.astype(jnp.bfloat16)
    hidden_rows = lax.all_gather(low_hidden, "tensor", axis=0, tiled=True)
    grad_out = jnp.einsum("gte,tgd->ed", mixed, hidden_rows, preferred_element_type=jnp.float32)
    grad_mixed = jnp.einsum(
        "tgd,ed->gte", hidden_rows, out_weight, preferred_element_type=jnp.float32
    ).astype(jnp.bfloat16)
    grad_heads = lax.map(
        attend_back,
        (
            split_heads[0],
            split_heads[1],
            split_heads[2],
            grad_mixed.reshape(seq_count, full_rows, heads_local, HEAD_DIM),
            log_total,
        ),
    )
    grad_projected = grad_heads.reshape(seq_count, 3, full_rows, local_width)
    grad_qkv = jnp.einsum(
        "tgd,gcte->cde", rows_one, grad_projected, preferred_element_type=jnp.float32
    )
    piece_rows = grad_projected
    grad_normed_one = lax.psum_scatter(
        jnp.einsum(
            "gcte,cde->tgd", piece_rows, qkv_weight, preferred_element_type=jnp.float32
        ).astype(jnp.bfloat16),
        "tensor",
        scatter_dimension=0,
        tiled=True,
    ).astype(jnp.float32)
    grad_input_norm, gain_one_grad, bias_one_grad = norm_back(
        grad_normed_one, normal_one, inverse_one, gain_one.astype(jnp.float32)
    )
    input_grad = (grad_hidden + grad_input_norm).astype(jnp.bfloat16)
    owned = (
        lax.psum_scatter(
            gain_one_grad.astype(jnp.bfloat16), "dp", scatter_dimension=0, tiled=True
        ).astype(jnp.float32),
        lax.psum_scatter(
            bias_one_grad.astype(jnp.bfloat16), "dp", scatter_dimension=0, tiled=True
        ).astype(jnp.float32),
        lax.psum_scatter(
            grad_qkv.astype(jnp.bfloat16), "dp", scatter_dimension=1, tiled=True
        ).astype(jnp.float32),
        lax.psum_scatter(
            grad_out.astype(jnp.bfloat16), "dp", scatter_dimension=1, tiled=True
        ).astype(jnp.float32),
        lax.psum_scatter(
            gain_two_grad.astype(jnp.bfloat16), "dp", scatter_dimension=0, tiled=True
        ).astype(jnp.float32),
        lax.psum_scatter(
            bias_two_grad.astype(jnp.bfloat16), "dp", scatter_dimension=0, tiled=True
        ).astype(jnp.float32),
        lax.psum_scatter(
            grad_up.astype(jnp.bfloat16), "dp", scatter_dimension=0, tiled=True
        ).astype(jnp.float32),
        lax.psum_scatter(
            grad_down.astype(jnp.bfloat16), "dp", scatter_dimension=1, tiled=True
        ).astype(jnp.float32),
    )
    norm_sums = lax.psum((owned[0], owned[1], owned[4], owned[5]), "tensor")
    return (
        block_out,
        input_grad,
        norm_sums[0],
        norm_sums[1],
        owned[2],
        owned[3],
        norm_sums[2],
        norm_sums[3],
        owned[6],
        owned[7],
    )


def solution(mesh):
    placed = (
        P("tensor", "dp", None),
        P("tensor", "dp", None),
        P("dp"),
        P("dp"),
        P(None, "dp", "tensor"),
        P("tensor", "dp"),
        P("dp"),
        P("dp"),
        P("dp", "tensor"),
        P("tensor", "dp"),
    )
    return jax.shard_map(
        on_device,
        mesh=mesh,
        in_specs=placed,
        out_specs=(
            P("tensor", "dp", None),
            P("tensor", "dp", None),
            P("dp"),
            P("dp"),
            P(None, "dp", "tensor"),
            P("tensor", "dp"),
            P("dp"),
            P("dp"),
            P("dp", "tensor"),
            P("tensor", "dp"),
        ),
        check_vma=False,
    )
```

profile of v0, /device:TPU:0, one launch (start us, length us, event | category | flops | bytes accessed | tf_op | source)
XLA Modules:
  0.0 1248.3 jit_solution(5901912760766693115)
XLA Ops:
  12.7 36.0 %all-reduce.11 = (bf16[1024]{0:T(1024)(128)(2,1)}, bf16[1024]{0:T(1024)(128)(2,1)}, bf16[1024]{0:T(1024)(128)(2,1)S(1)}, bf16[1024]{0:T(1024)(128)(2,1)S(1)}) all-reduce(bf16[1024]{0:T(1024)(128)(2,1)S(1)} %dynamic-update-slice.3, bf16[1024]{0:T(1024)(128)(2,1)S(1)} %dynamic-update-slice.2, ...), channel_id=1, replica_groups=mesh['dp'=16,'tensor'=2] {'dp'}, use_global_device_ids=true, to_apply=%add.3 | all-reduce | flops 4096 | bytes 16384
  57.9 52.4 %all-gather.9.cloned.1.call-done = bf16[1024,2,1024]{2,0,1:T(8,128)(2,1)} async-done(((bf16[512,2,1024]{2,0,1:T(8,128)(2,1)}), bf16[1024,2,1024]{2,0,1:T(8,128)(2,1)}) %all-gather.9.cloned.1.call-update) | async-done | bytes 4194320 | tf_op jit(solution)/shard_map/all_gather | solution.py:94
  110.3 47.4 %all-gather.11.cloned.1.call-done = bf16[3,1024,512]{2,1,0:T(8,128)(2,1)} async-done(((bf16[3,64,512]{2,1,0:T(8,128)(2,1)}), bf16[3,1024,512]{2,1,0:T(8,128)(2,1)}) %all-gather.11.cloned.1.call-update) | async-done | bytes 3145744 | tf_op jit(solution)/shard_map/all_gather | solution.py:79
  170.3 90.0 %while.22 = (s32[]{:T(128)}, bf16[2,1024,8,64]{1,3,2,0:T(8,128)(2,1)}, f32[2,8,1024,1]{2,1,3,0:T(8,128)S(1)}, bf16[2,1024,8,64]{1,3,2,0:T(8,128)(2,1)}, bf16[2,1...) while((s32[]{:T(128)}, bf16[2,1024,8,64]{1,3,2,0:T(8,128)(2,1)}, ...), condition=%wide.region_5.6_spmd, body=%wide.region_2.5_spmd.sunk | while | flops 2249711616 | bytes 117704816 | solution.py:102
  170.6 14.8 %fusion.145 = (f32[8,1024]{1,0:T(8,128)S(1)}, f32[8,1024,1024]{1,2,0:T(8,128)}) fusion(pred[1024,1024]{0,1:T(8,128)(4,1)S(1)} %iota_compare_fusion.4, bf16[2,1024,8,64]{1,3,2,0:T(8,128)(2,1)S(1)} %get-tuple-element.267, s32[]{:T(128)S(6)} %copy.93, bf16[2,1024,8,64]{1,3,2,0:T(8,128)(2,1)} %get-tuple-element.266), kind=kOutput, calls=%fused_computation.3.clone.1 | convolution fusion | flops 1098899456 | bytes 36733952 | tf_op jit(solution)/shard_map/while/body/eval_jaxpr/qhd,khd->hqk/dot_general | solution.py:35
  199.9 15.4 %fusion.147 = bf16[2,1024,8,64]{1,3,2,0:T(8,128)(2,1)} fusion(bf16[2,1024,8,64]{1,3,2,0:T(8,128)(2,1)} %get-tuple-element.256, s32[]{:T(128)S(6)} %copy.93, f32[8,1024,1024]{1,2,0:T(8,128)} %get-tuple-element.237, f32[8,1024]{1,0:T(8,128)S(1)} %fusion.146, f32[8,1024]{1,0:T(8,128)S(1)} %get-tuple-element.238, ...), kind=kOutput, calls=%fused_computation.9.clone.1 | convolution fusion | flops 1116209152 | bytes 36766720 | tf_op jit(solution)/shard_map/while/body/eval_jaxpr/hqk,khd->qhd/dot_general | solution.py:43
  215.7 14.7 %fusion.145 = (f32[8,1024]{1,0:T(8,128)S(1)}, f32[8,1024,1024]{1,2,0:T(8,128)}) fusion(pred[1024,1024]{0,1:T(8,128)(4,1)S(1)} %iota_compare_fusion.4, bf16[2,1024,8,64]{1,3,2,0:T(8,128)(2,1)S(1)} %get-tuple-element.267, s32[]{:T(128)S(6)} %copy.93, bf16[2,1024,8,64]{1,3,2,0:T(8,128)(2,1)} %get-tuple-element.266), kind=kOutput, calls=%fused_computation.3.clone.1 | convolution fusion | flops 1098899456 | bytes 36733952 | tf_op jit(solution)/shard_map/while/body/eval_jaxpr/qhd,khd->hqk/dot_general | solution.py:35
  244.8 15.4 %fusion.147 = bf16[2,1024,8,64]{1,3,2,0:T(8,128)(2,1)} fusion(bf16[2,1024,8,64]{1,3,2,0:T(8,128)(2,1)} %get-tuple-element.256, s32[]{:T(128)S(6)} %copy.93, f32[8,1024,1024]{1,2,0:T(8,128)} %get-tuple-element.237, f32[8,1024]{1,0:T(8,128)S(1)} %fusion.146, f32[8,1024]{1,0:T(8,128)S(1)} %get-tuple-element.238, ...), kind=kOutput, calls=%fused_computation.9.clone.1 | convolution fusion | flops 1116209152 | bytes 36766720 | tf_op jit(solution)/shard_map/while/body/eval_jaxpr/hqk,khd->qhd/dot_general | solution.py:43
  268.8 52.6 %reduce-scatter.8.cloned.1.call-done = bf16[512,2,1024]{2,0,1:T(8,128)(2,1)} async-done(((bf16[1024,2,1024]{2,0,1:T(8,128)(2,1)}), bf16[512,2,1024]{2,0,1:T(8,128)(2,1)}) %reduce-scatter.8.cloned.1.call-update) | async-done | bytes 2097168 | tf_op jit(solution)/shard_map/reduce_scatter | solution.py:105
  331.3 42.8 %all-gather.17.cloned.1.call-done = bf16[1024,2048]{1,0:T(8,128)(2,1)} async-done(((bf16[64,2048]{1,0:T(8,128)(2,1)}), bf16[1024,2048]{1,0:T(8,128)(2,1)}) %all-gather.17.cloned.1.call-update) | async-done | bytes 4194320 | tf_op jit(solution)/shard_map/all_gather | solution.py:83
  374.2 56.7 %all-gather.15.cloned.1.call-done = bf16[1024,2,1024]{2,0,1:T(8,128)(2,1)} async-done(((bf16[512,2,1024]{2,0,1:T(8,128)(2,1)}), bf16[1024,2,1024]{2,0,1:T(8,128)(2,1)}) %all-gather.15.cloned.1.call-update) | async-done | bytes 4194320 | tf_op jit(solution)/shard_map/all_gather | solution.py:117
  430.9 15.3 %fusion.93 = f32[1024,2,2048]{2,0,1:T(8,128)} fusion(bf16[1024,2,1024]{2,0,1:T(8,128)(2,1)} %all-gather.15.cloned.1.call-done, bf16[1024,2048]{1,0:T(8,128)(2,1)} %all-gather.17.cloned.1.call-done), kind=kOutput, calls=%fused_computation.116 | convolution fusion | flops 8589934592 | bytes 25165824 | tf_op jit(solution)/shard_map/tgd,df->tgf/dot_general | solution.py:118
  446.2 43.1 %all-gather.21.cloned.1.call-done = bf16[1024,2,1024]{2,0,1:T(8,128)(2,1)} async-done(((bf16[512,2,1024]{2,0,1:T(8,128)(2,1)}), bf16[1024,2,1024]{2,0,1:T(8,128)(2,1)}) %all-gather.21.cloned.1.call-update) | async-done | bytes 4194320 | tf_op jit(solution)/shard_map/all_gather | solution.py:130
  489.3 53.0 %all-gather.19.cloned.1.call-done = bf16[2048,1024]{0,1:T(8,128)(2,1)} async-done(((bf16[2048,64]{0,1:T(8,128)(2,1)}), bf16[2048,1024]{0,1:T(8,128)(2,1)}) %all-gather.19.cloned.1.call-update) | async-done | bytes 4194320 | tf_op jit(solution)/shard_map/all_gather | solution.py:84
  542.3 22.3 %fusion.58 = bf16[1024,2,2048]{2,0,1:T(8,128)(2,1)S(1)} fusion(f32[1024,2,2048]{2,0,1:T(8,128)} %fusion.93, bf16[1024,2,1024]{2,0,1:T(8,128)(2,1)} %all-gather.21.cloned.1.call-done, bf16[2048,1024]{0,1:T(8,128)(2,1)} %all-gather.19.cloned.1.call-done), kind=kOutput, calls=%fused_computation.68 | convolution fusion | flops 8673820672 | bytes 33554432 | tf_op jit(solution)/shard_map/tgd,fd->tgf/dot_general | solution.py:132
  578.8 52.9 %reduce-scatter.12.cloned.1.call-done = bf16[512,2,1024]{2,0,1:T(8,128)(2,1)} async-done(((bf16[1024,2,1024]{2,0,1:T(8,128)(2,1)}), bf16[512,2,1024]{2,0,1:T(8,128)(2,1)}) %reduce-scatter.12.cloned.1.call-update) | async-done | bytes 2097168 | tf_op jit(solution)/shard_map/reduce_scatter | solution.py:139
  639.5 16.0 %bitcast_convert_fusion = bf16[2048,1024]{0,1:T(8,128)(2,1)} fusion(bf16[1024,2,1024]{2,0,1:T(8,128)(2,1)} %all-gather.21.cloned.1.call-done, f32[1024,2,2048]{2,0,1:T(8,128)} %fusion.93), kind=kOutput, calls=%fused_computation.70 | convolution fusion | flops 8629780480 | bytes 25165824 | tf_op jit(solution)/shard_map/tgf,tgd->fd/dot_general | solution.py:131
  669.8 26.6 %all-gather.23.cloned.1.call-done = bf16[1024,2,1024]{2,0,1:T(8,128)(2,1)} async-done(((bf16[512,2,1024]{2,0,1:T(8,128)(2,1)}), bf16[1024,2,1024]{2,0,1:T(8,128)(2,1)}) %all-gather.23.cloned.1.call-update) | async-done | bytes 4194320 | tf_op jit(solution)/shard_map/all_gather | solution.py:152
  702.3 220.0 %while.23 = (s32[]{:T(128)}, bf16[2,3,1024,8,64]{2,4,3,1,0:T(8,128)(2,1)}, bf16[2,1024,8,64]{1,3,2,0:T(8,128)(2,1)S(1)}, bf16[2,1024,8,64]{1,3,2,0:T(8,128)(2,1)...) while((s32[]{:T(128)}, ...), condition=%wide.region_15.16_spmd, body=%wide.region_13.15_spmd.sunk | while | flops 5507637248 | bytes 272861280 | solution.py:157
  703.1 16.0 %fusion.156 = f32[8,1024,1024]{1,2,0:T(8,128)} fusion(bf16[2,1024,8,64]{1,3,2,0:T(8,128)(2,1)} %get-tuple-element.288, s32[]{:T(128)S(6)} %copy.101, bf16[2,1024,8,64]{1,3,2,0:T(8,128)(2,1)S(1)} %get-tuple-element.287), kind=kOutput, calls=%fused_computation.41.clone.1 | convolution fusion | flops 1073741824 | bytes 35652608 | tf_op jit(solution)/shard_map/while/body/eval_jaxpr/qhd,khd->hqk/dot_general | solution.py:51
  719.1 16.4 %fusion.157 = bf16[1,1,1024,8,64]{2,4,3,1,0:T(8,128)(2,1)} fusion(f32[8,1024,1024]{1,2,0:T(8,128)} %fusion.156, f32[8,1024]{1,0:T(8,128)S(1)} %dynamic-slice_bitcast_fusion.2, pred[1024,1024]{0,1:T(8,128)(4,1)S(1)} %iota_compare_fusion.5, bf16[2,1024,8,64]{1,3,2,0:T(8,128)(2,1)} %get-tuple-element.290, s32[]{:T(128)S(6)} %copy.101), kind=kOutput, calls=%fused_computation.35.clone.1 | convolution fusion | flops 1107820544 | bytes 36732932 | tf_op jit(solution)/shard_map/while/body/eval_jaxpr/hqk,qhd->khd/dot_general | solution.py:55
  735.5 24.0 %multiply_reduce_fusion.3 = (f32[8,1024]{1,0:T(8,128)S(1)}, f32[8,1024,1024]{1,2,0:T(8,128)}) fusion(f32[8,1024,1024]{1,2,0:T(8,128)} %fusion.156, f32[8,1024]{1,0:T(8,128)S(1)} %dynamic-slice_bitcast_fusion.2, pred[1024,1024]{0,1:T(8,128)(4,1)S(1)} %iota_compare_fusion.5, bf16[2,1024,8,64]{1,3,2,0:T(8,128)(2,1)} %get-tuple-element.291, ...), kind=kOutput, calls=%fused_computation.23.clone.1 | convolution fusion | flops 1115676672 | bytes 70321152 | tf_op jit(solution)/shard_map/while/body/eval_jaxpr/qhd,khd->hqk/dot_general | solution.py:58
  759.5 29.1 %multiply_convert_fusion.7 = bf16[8,1024,1024]{1,2,0:T(8,128)(2,1)} fusion(f32[8,1024,1024]{1,2,0:T(8,128)} %get-tuple-element.246, f32[8,1024,1024]{1,2,0:T(8,128)} %fusion.156, f32[8,1024]{1,0:T(8,128)S(1)} %get-tuple-element.247, f32[8,1024]{1,0:T(8,128)S(1)} %dynamic-slice_bitcast_fusion.2, pred[1024,1024]{0,1:T(8,128)(4,1)S(1)} %iota_compare_fusion.5), kind=kLoop, calls=%fused_computation.22.clone.1 | loop fusion | flops 50331648 | bytes 85000192 | tf_op jit(solution)/shard_map/while/body/eval_jaxpr/convert_element_type | solution.py:62
  829.0 16.2 %fusion.157 = bf16[1,1,1024,8,64]{2,4,3,1,0:T(8,128)(2,1)} fusion(f32[8,1024,1024]{1,2,0:T(8,128)} %fusion.156, f32[8,1024]{1,0:T(8,128)S(1)} %dynamic-slice_bitcast_fusion.2, pred[1024,1024]{0,1:T(8,128)(4,1)S(1)} %iota_compare_fusion.5, bf16[2,1024,8,64]{1,3,2,0:T(8,128)(2,1)} %get-tuple-element.290, s32[]{:T(128)S(6)} %copy.101), kind=kOutput, calls=%fused_computation.35.clone.1 | convolution fusion | flops 1107820544 | bytes 36732932 | tf_op jit(solution)/shard_map/while/body/eval_jaxpr/hqk,qhd->khd/dot_general | solution.py:55
  845.2 23.8 %multiply_reduce_fusion.3 = (f32[8,1024]{1,0:T(8,128)S(1)}, f32[8,1024,1024]{1,2,0:T(8,128)}) fusion(f32[8,1024,1024]{1,2,0:T(8,128)} %fusion.156, f32[8,1024]{1,0:T(8,128)S(1)} %dynamic-slice_bitcast_fusion.2, pred[1024,1024]{0,1:T(8,128)(4,1)S(1)} %iota_compare_fusion.5, bf16[2,1024,8,64]{1,3,2,0:T(8,128)(2,1)} %get-tuple-element.291, ...), kind=kOutput, calls=%fused_computation.23.clone.1 | convolution fusion | flops 1115676672 | bytes 70321152 | tf_op jit(solution)/shard_map/while/body/eval_jaxpr/qhd,khd->hqk/dot_general | solution.py:58
  869.0 28.5 %multiply_convert_fusion.7 = bf16[8,1024,1024]{1,2,0:T(8,128)(2,1)} fusion(f32[8,1024,1024]{1,2,0:T(8,128)} %get-tuple-element.246, f32[8,1024,1024]{1,2,0:T(8,128)} %fusion.156, f32[8,1024]{1,0:T(8,128)S(1)} %get-tuple-element.247, f32[8,1024]{1,0:T(8,128)S(1)} %dynamic-slice_bitcast_fusion.2, pred[1024,1024]{0,1:T(8,128)(4,1)S(1)} %iota_compare_fusion.5), kind=kLoop, calls=%fused_computation.22.clone.1 | loop fusion | flops 50331648 | bytes 85000192 | tf_op jit(solution)/shard_map/while/body/eval_jaxpr/convert_element_type | solution.py:62
  955.9 16.6 %fusion.104 = bf16[1024,2,1024]{2,0,1:T(8,128)(2,1)} fusion(bf16[2048,1024]{0,1:T(8,128)(2,1)} %all-gather.19.cloned.1.call-done, f32[1024,2,2048]{2,0,1:T(8,128)} %fusion.93), kind=kOutput, calls=%fused_computation.128 | convolution fusion | flops 8629780480 | bytes 25165824 | tf_op jit(solution)/shard_map/tgf,fd->tgd/dot_general | solution.py:122
  978.9 70.7 %all-reduce.14.cloned.1.call-done = bf16[3,1024,512]{2,0,1:T(4,128)(2,1)} async-done(((bf16[3,1024,512]{2,0,1:T(4,128)(2,1)}), bf16[3,1024,512]{2,0,1:T(4,128)(2,1)}) %all-reduce.14.cloned.1.call-update) | async-done | bytes 3145744
  1051.5 59.0 %reduce-scatter.16.cloned.1.call-done = bf16[512,64]{0,1:T(8,128)(2,1)} async-done(((bf16[512,1024]{0,1:T(8,128)(2,1)}), bf16[512,64]{0,1:T(8,128)(2,1)}) %reduce-scatter.16.cloned.1.call-update) | async-done | bytes 65552 | tf_op jit(solution)/shard_map/reduce_scatter | solution.py:194
  1111.9 54.0 %reduce-scatter.14.cloned.1.call-done = bf16[512,2,1024]{2,0,1:T(8,128)(2,1)} async-done(((bf16[1024,2,1024]{2,0,1:T(8,128)(2,1)}), bf16[512,2,1024]{2,0,1:T(8,128)(2,1)}) %reduce-scatter.14.cloned.1.call-update) | async-done | bytes 2097168 | tf_op jit(solution)/shard_map/reduce_scatter | solution.py:172
  1171.5 33.9 %all-reduce.10 = (bf16[1024]{0:T(1024)(128)(2,1)S(1)}, bf16[1024]{0:T(1024)(128)(2,1)S(1)}, bf16[1024]{0:T(1024)(128)(2,1)S(1)}, bf16[1024]{0:T(1024)(128)(2,1)S(1)}) all-reduce(bf16[1024]{0:T(1024)(128)(2,1)S(1)} %get-tuple-element.105, bf16[1024]{0:T(1024)(128)(2,1)S(1)} %reduce_sum.141, ...), channel_id=6, replica_groups=mesh['dp'=16,'tensor'=2] {'dp'}, use_global_device_ids=true, to_apply=%region_20.21.clone | all-reduce | flops 4096 | bytes 16384
  1205.7 16.8 %reduce-scatter.10.cloned.1.call-done = bf16[512,2,1024]{2,0,1:T(8,128)(2,1)} async-done(((bf16[1024,2,1024]{2,0,1:T(8,128)(2,1)}), bf16[512,2,1024]{2,0,1:T(8,128)(2,1)}) %reduce-scatter.10.cloned.1.call-update) | async-done | bytes 2097168 | tf_op jit(solution)/shard_map/reduce_scatter | solution.py:121
  (178 shorter events, 248.9 us)
Async XLA Ops:
  7.2 46.7 %copy-start = (bf16[512,2,1024]{2,1,0:T(2,128)(2,1)S(1)}, bf16[512,2,1024]{2,1,0:T(2,128)(2,1)}, u32[]{:S(2)}) copy-start(bf16[512,2,1024]{2,1,0:T(2,128)(2,1)} %param.14) | copy-start | bytes 6291460
  7.2 103.1 %all-gather.9.cloned.1.call-start = ((), (), s32[]{:S(2)}) async-start(), calls=%async_computation.7 | async-start | bytes 6291456 | tf_op jit(solution)/shard_map/all_gather | solution.py:94
  56.1 101.6 %all-gather.11.cloned.1.call-start = ((), (), s32[]{:S(2)}) async-start(), calls=%async_computation.8 | async-start | bytes 3342336 | tf_op jit(solution)/shard_map/all_gather | solution.py:79
  56.9 203.5 %all-gather.13.cloned.1.call-start = ((), (), s32[]{:S(2)}) async-start(), calls=%async_computation.9 | async-start | bytes 1114112 | tf_op jit(solution)/shard_map/all_gather | solution.py:80
  57.6 263.7 %reduce-scatter.8.cloned.1.call-start = ((), (), s32[]{:S(2)}) async-start(), calls=%async_computation.10 | async-start | bytes 6291456 | tf_op jit(solution)/shard_map/reduce_scatter | solution.py:105
  268.1 53.3 %copy-start.1 = (bf16[512,2,1024]{2,1,0:T(2,128)(2,1)S(1)}, bf16[512,2,1024]{2,1,0:T(2,128)(2,1)}, u32[]{:S(2)}) copy-start(bf16[512,2,1024]{2,1,0:T(2,128)(2,1)} %param.14) | copy-start | bytes 6291460
  268.1 106.1 %all-gather.17.cloned.1.call-start = ((), (), s32[]{:S(2)}) async-start(), calls=%async_computation.12 | async-start | bytes 4456448 | tf_op jit(solution)/shard_map/all_gather | solution.py:83
  268.7 162.2 %all-gather.15.cloned.1.call-start = ((), (), s32[]{:S(2)}) async-start(), calls=%async_computation.11 | async-start | bytes 6291456 | tf_op jit(solution)/shard_map/all_gather | solution.py:117
  268.8 367.8 %copy-start.12 = (f32[1024]{0:T(1024)}, f32[1024]{0:T(1024)S(1)}, u32[]{:S(2)}) copy-start(f32[1024]{0:T(1024)S(1)} %convert_element_type.162) | copy-start | bytes 12292
  323.8 312.7 %copy-start.10 = (f32[512,2]{0,1:T(2,128)}, f32[512,2]{0,1:T(2,128)S(1)}, u32[]{:S(2)}) copy-start(f32[512,2]{0,1:T(2,128)S(1)} %broadcast_multiply_fusion.4) | copy-start | bytes 12292
  324.8 311.8 %copy-start.14 = (f32[512,2]{0,1:T(2,128)}, f32[512,2]{0,1:T(2,128)S(1)}, u32[]{:S(2)}) copy-start(f32[512,2]{0,1:T(2,128)S(1)} %add_rsqrt_fusion) | copy-start | bytes 12292
  326.9 162.4 %all-gather.21.cloned.1.call-start = ((), (), s32[]{:S(2)}) async-start(), calls=%async_computation.15 | async-start | bytes 6291456 | tf_op jit(solution)/shard_map/all_gather | solution.py:130
  330.5 211.8 %all-gather.19.cloned.1.call-start = ((), (), s32[]{:S(2)}) async-start(), calls=%async_computation.13 | async-start | bytes 4456448 | tf_op jit(solution)/shard_map/all_gather | solution.py:84
  331.3 300.4 %reduce-scatter.12.cloned.1.call-start = ((), (), s32[]{:S(2)}) async-start(), calls=%async_computation.16 | async-start | bytes 6291456 | tf_op jit(solution)/shard_map/reduce_scatter | solution.py:139
  578.8 117.6 %all-gather.23.cloned.1.call-start = ((), (), s32[]{:S(2)}) async-start(), calls=%async_computation.17 | async-start | bytes 6291456 | tf_op jit(solution)/shard_map/all_gather | solution.py:152
  639.5 333.9 %reduce-scatter.20.cloned.1.call-start = ((), (), s32[]{:S(2)}) async-start(), calls=%async_computation.21 | async-start | bytes 4456448 | tf_op jit(solution)/shard_map/reduce_scatter | solution.py:206
  655.6 319.6 %reduce-scatter.18.cloned.1.call-start = ((), (), s32[]{:S(2)}) async-start(), calls=%async_computation.20 | async-start | bytes 4456448 | tf_op jit(solution)/shard_map/reduce_scatter | solution.py:203
  669.7 32.6 %copy-start.4 = (bf16[2,1024,8,64]{1,3,2,0:T(8,128)(2,1)S(1)}, bf16[2,1024,8,64]{1,3,2,0:T(8,128)(2,1)}, u32[]{:S(2)}) copy-start(bf16[2,1024,8,64]{1,3,2,0:T(8,128)(2,1)} %copy-done.3) | copy-start | bytes 6291460
  669.7 379.9 %all-reduce.14.cloned.1.call-start = ((), (), s32[]{:S(2)}) async-start(), calls=%async_computation.22 | async-start | bytes 8388608
  938.2 172.3 %reduce-scatter.16.cloned.1.call-start = ((), (), s32[]{:S(2)}) async-start(), calls=%async_computation.19 | async-start | bytes 1114112 | tf_op jit(solution)/shard_map/reduce_scatter | solution.py:194
  944.6 221.4 %reduce-scatter.14.cloned.1.call-start = ((), (), s32[]{:S(2)}) async-start(), calls=%async_computation.18 | async-start | bytes 6291456 | tf_op jit(solution)/shard_map/reduce_scatter | solution.py:172
  955.8 266.7 %reduce-scatter.10.cloned.1.call-start = ((), (), s32[]{:S(2)}) async-start(), calls=%async_computation.14 | async-start | bytes 6291456 | tf_op jit(solution)/shard_map/reduce_scatter | solution.py:121
  972.5 195.4 %copy-start.2 = (bf16[512,2,1024]{2,1,0:T(2,128)(2,1)S(1)}, bf16[512,2,1024]{2,1,0:T(2,128)(2,1)}, u32[]{:S(2)}) copy-start(bf16[512,2,1024]{2,1,0:T(2,128)(2,1)} %param.14) | copy-start | bytes 6291460
  972.5 195.4 %copy-start.17 = (f32[512,2]{0,1:T(2,128)S(1)}, f32[512,2]{0,1:T(2,128)}, u32[]{:S(2)}) copy-start(f32[512,2]{0,1:T(2,128)} %copy-done.16) | copy-start | bytes 12292
  972.5 195.4 %copy-start.19 = (f32[1024]{0:T(1024)S(1)}, f32[1024]{0:T(1024)}, u32[]{:S(2)}) copy-start(f32[1024]{0:T(1024)} %copy-done.18) | copy-start | bytes 12292
  972.5 195.4 %copy-start.21 = (f32[512,2]{0,1:T(2,128)S(1)}, f32[512,2]{0,1:T(2,128)}, u32[]{:S(2)}) copy-start(f32[512,2]{0,1:T(2,128)} %copy-done.20) | copy-start | bytes 12292
  978.9 192.6 %copy-start.26 = (bf16[1024]{0:T(1024)(128)(2,1)S(1)}, bf16[1024]{0:T(1024)(128)(2,1)}, u32[]{:S(2)}) copy-start(bf16[1024]{0:T(1024)(128)(2,1)} %get-tuple-element.103) | copy-start | bytes 6148
  978.9 243.6 %copy-start.11 = (f32[512,2]{0,1:T(2,128)S(1)}, f32[512,2]{0,1:T(2,128)}, u32[]{:S(2)}) copy-start(f32[512,2]{0,1:T(2,128)} %copy-done.10) | copy-start | bytes 12292
  978.9 243.6 %copy-start.13 = (f32[1024]{0:T(1024)S(1)}, f32[1024]{0:T(1024)}, u32[]{:S(2)}) copy-start(f32[1024]{0:T(1024)} %copy-done.12) | copy-start | bytes 12292
  978.9 243.6 %copy-start.15 = (f32[512,2]{0,1:T(2,128)S(1)}, f32[512,2]{0,1:T(2,128)}, u32[]{:S(2)}) copy-start(f32[512,2]{0,1:T(2,128)} %copy-done.14) | copy-start | bytes 12292
  978.9 243.6 %copy-start.23 = (f32[512,2]{0,1:T(2,128)S(1)}, f32[512,2]{0,1:T(2,128)}, u32[]{:S(2)}) copy-start(f32[512,2]{0,1:T(2,128)} %copy-done.22) | copy-start | bytes 12292
  978.9 243.6 %copy-start.25 = (f32[512,2]{0,1:T(2,128)S(1)}, f32[512,2]{0,1:T(2,128)}, u32[]{:S(2)}) copy-start(f32[512,2]{0,1:T(2,128)} %copy-done.24) | copy-start | bytes 12292
  (18 other events, 124.0 us)
Sparse Core Ops, SparseCore 0:
  56.3 53.9 all-gather.8
  112.5 45.2 all-gather.10
  159.9 36.7 all-gather.12
  268.2 53.0 reduce-scatter.7
  323.6 50.5 all-gather.16
  375.6 55.2 all-gather.14
  432.5 56.7 all-gather.20
  491.7 50.5 all-gather.18
  578.9 52.7 reduce-scatter.11
  639.6 56.7 all-gather.22
  700.3 72.4 reduce-scatter.19
  777.0 71.4 reduce-scatter.17
  938.3 111.2 all-reduce.13
  1054.1 56.2 reduce-scatter.15
  1112.6 53.3 reduce-scatter.13
  1168.2 54.2 reduce-scatter.9
where the time goes:
time: 1250 us
  waiting for transfers between devices  631 us (50%)
  matrix products  359 us (29%)
  other arithmetic  135 us (11%)
  blocking collectives  75.3 us (6%)
  local copies, waits for them, and re-layouts  30.2 us (2%)
  between operations  16.1 us (1%)
    unnamed x17, waiting for transfers between devices  73.5 us
    unnamed x2, blocking collectives  69.9 us
    reduce_scatter x1, waiting for transfers between devices, on_device(): lax.psum_scatter(grad_out.astype(jnp.bfloat16), 'dp', scatter_dimension=1...  59 us
    convert_element_type x2, other arithmetic, attend_back(): grad_scores = (shares * (grad_shares - inner)).astype(jnp.bfloat16)  57.6 us
    all_gather x1, waiting for transfers between devices, on_device(): rows_two = lax.all_gather(low_two, 'tensor', axis=0, tiled=True)  56.7 us
    reduce_scatter x1, waiting for transfers between devices, on_device(): lax.psum_scatter(jnp.einsum('gcte,cde->tgd', piece_rows, qkv_weight, pref...  54 us
    all_gather x1, waiting for transfers between devices, on_device(): lax.all_gather(w_down, 'dp', axis=1, tiled=True)  53 us
    reduce_scatter x1, waiting for transfers between devices, on_device(): lax.psum_scatter(jnp.einsum('tgf,df->tgd', piece_rows, up_weight, preferr...  52.9 us
  transfers between devices with their start and end apart: 16, of which 13 were waited for; matrix products, arithmetic and copies ran while one was open for 36% of the time, Pallas kernels for 0%

commit v1 on v0

--- a/solution.py
+++ b/solution.py
@@ -5,6 +5,18 @@
 
 HEAD_DIM = 64
 EPSILON = 1e-05
+
+
+def collect(x, axis, dim):
+    ways, here, step = (lax.axis_size(axis), lax.axis_index(axis), x.shape[dim])
+    line, have = (x, 1)
+    while have < ways:
+        line = jnp.concatenate(
+            [line, lax.ppermute(line, axis, [(d, (d - have) % ways) for d in range(ways)])],
+            axis=dim,
+        )
+        have = 2 * have
+    return jnp.roll(line, here * step, axis=dim)
 
 
 def norm_rows(values, norm_gain, norm_bias):
@@ -127,7 +139,7 @@
         tiled=True,
     ).astype(jnp.float32)
     block_out = (hidden + block_sum).astype(jnp.bfloat16)
-    grad_rows = lax.all_gather(d_out, "tensor", axis=0, tiled=True)
+    grad_rows = collect(d_out, "tensor", 0)
     grad_down = jnp.einsum("tgf,tgd->fd", active, grad_rows, preferred_element_type=jnp.float32)
     grad_active = jnp.einsum(
         "tgd,fd->tgf", grad_rows, down_weight, preferred_element_type=jnp.float32

time: 1250 us -> 1190 us (0.952)
  waiting for transfers between devices: 631 us -> 564 us
    ppermute x0 -> x1, waiting for transfers between devices: none -> 47.4 us  [collect(): lax.ppermute(line, axis, [(d, (d - have) % ways) for d in range(ways)])]
    all_gather x1 -> x0, waiting for transfers between devices: 43.1 us -> none  [on_device(): grad_rows = lax.all_gather(d_out, 'tensor', axis=0, tiled=True)]
    all_gather x1, waiting for transfers between devices: 42.8 us -> 0.01 us  [on_device(): lax.all_gather(w_up, 'dp', axis=0, tiled=True)]
    all_gather x1, waiting for transfers between devices: 53 us -> 37.7 us  [on_device(): lax.all_gather(w_down, 'dp', axis=1, tiled=True)]
    all_gather x1, waiting for transfers between devices: 56.7 us -> 43.9 us  [on_device(): rows_two = lax.all_gather(low_two, 'tensor', axis=0, tiled=True)]
    unnamed x17 -> x16, waiting for transfers between devices: 73.5 us -> 73.2 us
  transfers between devices with their start and end apart: 16 -> 16, of which waited for: 13 -> 12; matrix products, arithmetic and copies ran while one was open for 36% -> 38% of each run, Pallas kernels for 0% -> 0%
where the time goes in v1:
time: 1190 us
  waiting for transfers between devices  564 us (47%)
  matrix products  359 us (30%)
  other arithmetic  144 us (12%)
  blocking collectives  75.2 us (6%)
  local copies, waits for them, and re-layouts  30.1 us (3%)
  between operations  16 us (1%)
    unnamed x16, waiting for transfers between devices  73.2 us
    unnamed x2, blocking collectives  69.8 us
    reduce_scatter x1, waiting for transfers between devices, on_device(): lax.psum_scatter(grad_out.astype(jnp.bfloat16), 'dp', scatter_dimension=1...  59.1 us
    convert_element_type x2, other arithmetic, attend_back(): grad_scores = (shares * (grad_shares - inner)).astype(jnp.bfloat16)  57.5 us
    reduce_scatter x1, waiting for transfers between devices, on_device(): lax.psum_scatter(jnp.einsum('gcte,cde->tgd', piece_rows, qkv_weight, pref...  54 us
    reduce_scatter x1, waiting for transfers between devices, on_device(): lax.psum_scatter(jnp.einsum('tgf,df->tgd', piece_rows, up_weight, preferr...  52.9 us
    reduce_scatter x1, waiting for transfers between devices, on_device(): lax.psum_scatter(jnp.einsum('gte,ed->tgd', piece_rows, out_weight, prefer...  52.6 us
    all_gather x1, waiting for transfers between devices, on_device(): rows_one = lax.all_gather(low_one, 'tensor', axis=0, tiled=True)  52.3 us
  transfers between devices with their start and end apart: 16, of which 12 were waited for; matrix products, arithmetic and copies ran while one was open for 38% of the time, Pallas kernels for 0%

profile of v1, /device:TPU:0, one launch (start us, length us, event | category | flops | bytes accessed | tf_op | source)
XLA Modules:
  0.0 1190.3 jit_solution(13021504561515831622)
XLA Ops:
  12.7 36.0 %all-reduce.11 = (bf16[1024]{0:T(1024)(128)(2,1)}, bf16[1024]{0:T(1024)(128)(2,1)}, bf16[1024]{0:T(1024)(128)(2,1)S(1)}, bf16[1024]{0:T(1024)(128)(2,1)S(1)}) all-reduce(bf16[1024]{0:T(1024)(128)(2,1)S(1)} %dynamic-update-slice.3, bf16[1024]{0:T(1024)(128)(2,1)S(1)} %dynamic-update-slice.2, ...), channel_id=1, replica_groups=mesh['dp'=16,'tensor'=2] {'dp'}, use_global_device_ids=true, to_apply=%add.3 | all-reduce | flops 4096 | bytes 16384
  58.0 52.3 %all-gather.8.cloned.1.call-done = bf16[1024,2,1024]{2,0,1:T(8,128)(2,1)} async-done(((bf16[512,2,1024]{2,0,1:T(8,128)(2,1)}), bf16[1024,2,1024]{2,0,1:T(8,128)(2,1)}) %all-gather.8.cloned.1.call-update) | async-done | bytes 4194320 | tf_op jit(solution)/shard_map/all_gather | solution.py:106
  110.3 47.4 %all-gather.10.cloned.1.call-done = bf16[3,1024,512]{2,1,0:T(8,128)(2,1)} async-done(((bf16[3,64,512]{2,1,0:T(8,128)(2,1)}), bf16[3,1024,512]{2,1,0:T(8,128)(2,1)}) %all-gather.10.cloned.1.call-update) | async-done | bytes 3145744 | tf_op jit(solution)/shard_map/all_gather | solution.py:91
  170.4 90.4 %while.22 = (s32[]{:T(128)}, bf16[2,1024,8,64]{1,3,2,0:T(8,128)(2,1)}, f32[2,8,1024,1]{2,1,3,0:T(8,128)S(1)}, bf16[2,1024,8,64]{1,3,2,0:T(8,128)(2,1)}, bf16[2,1...) while((s32[]{:T(128)}, bf16[2,1024,8,64]{1,3,2,0:T(8,128)(2,1)}, ...), condition=%wide.region_5.6_spmd, body=%wide.region_2.5_spmd.sunk | while | flops 2249711616 | bytes 117704816 | solution.py:114
  170.7 14.9 %fusion.148 = (f32[8,1024]{1,0:T(8,128)S(1)}, f32[8,1024,1024]{1,2,0:T(8,128)}) fusion(pred[1024,1024]{0,1:T(8,128)(4,1)S(1)} %iota_compare_fusion.4, bf16[2,1024,8,64]{1,3,2,0:T(8,128)(2,1)S(1)} %get-tuple-element.267, s32[]{:T(128)S(6)} %copy.97, bf16[2,1024,8,64]{1,3,2,0:T(8,128)(2,1)} %get-tuple-element.266), kind=kOutput, calls=%fused_computation.3.clone.1 | convolution fusion | flops 1098899456 | bytes 36733952 | tf_op jit(solution)/shard_map/while/body/eval_jaxpr/qhd,khd->hqk/dot_general | solution.py:47
  200.0 15.4 %fusion.150 = bf16[2,1024,8,64]{1,3,2,0:T(8,128)(2,1)} fusion(bf16[2,1024,8,64]{1,3,2,0:T(8,128)(2,1)} %get-tuple-element.256, s32[]{:T(128)S(6)} %copy.97, f32[8,1024,1024]{1,2,0:T(8,128)} %get-tuple-element.237, f32[8,1024]{1,0:T(8,128)S(1)} %fusion.149, f32[8,1024]{1,0:T(8,128)S(1)} %get-tuple-element.238, ...), kind=kOutput, calls=%fused_computation.9.clone.1 | convolution fusion | flops 1116209152 | bytes 36766720 | tf_op jit(solution)/shard_map/while/body/eval_jaxpr/hqk,khd->qhd/dot_general | solution.py:55
  215.7 14.7 %fusion.148 = (f32[8,1024]{1,0:T(8,128)S(1)}, f32[8,1024,1024]{1,2,0:T(8,128)}) fusion(pred[1024,1024]{0,1:T(8,128)(4,1)S(1)} %iota_compare_fusion.4, bf16[2,1024,8,64]{1,3,2,0:T(8,128)(2,1)S(1)} %get-tuple-element.267, s32[]{:T(128)S(6)} %copy.97, bf16[2,1024,8,64]{1,3,2,0:T(8,128)(2,1)} %get-tuple-element.266), kind=kOutput, calls=%fused_computation.3.clone.1 | convolution fusion | flops 1098899456 | bytes 36733952 | tf_op jit(solution)/shard_map/while/body/eval_jaxpr/qhd,khd->hqk/dot_general | solution.py:47
  244.8 15.4 %fusion.150 = bf16[2,1024,8,64]{1,3,2,0:T(8,128)(2,1)} fusion(bf16[2,1024,8,64]{1,3,2,0:T(8,128)(2,1)} %get-tuple-element.256, s32[]{:T(128)S(6)} %copy.97, f32[8,1024,1024]{1,2,0:T(8,128)} %get-tuple-element.237, f32[8,1024]{1,0:T(8,128)S(1)} %fusion.149, f32[8,1024]{1,0:T(8,128)S(1)} %get-tuple-element.238, ...), kind=kOutput, calls=%fused_computation.9.clone.1 | convolution fusion | flops 1116209152 | bytes 36766720 | tf_op jit(solution)/shard_map/while/body/eval_jaxpr/hqk,khd->qhd/dot_general | solution.py:55
  269.1 52.6 %reduce-scatter.8.cloned.1.call-done = bf16[512,2,1024]{2,0,1:T(8,128)(2,1)} async-done(((bf16[1024,2,1024]{2,0,1:T(8,128)(2,1)}), bf16[512,2,1024]{2,0,1:T(8,128)(2,1)}) %reduce-scatter.8.cloned.1.call-update) | async-done | bytes 2097168 | tf_op jit(solution)/shard_map/reduce_scatter | solution.py:117
  331.8 47.4 %collective-permute-done = bf16[512,2,1024]{2,0,1:T(8,128)(2,1)} collective-permute-done((bf16[512,2,1024]{2,0,1:T(8,128)(2,1)}, bf16[512,2,1024]{2,0,1:T(8,128)(2,1)}, u32[]{:S(2)}, u32[]{:S(2)}) %collective-permute-start) | collective-permute-done | bytes 2097184 | tf_op jit(solution)/shard_map/ppermute | solution.py:15
  387.5 43.9 %all-gather.14.cloned.1.call-done = bf16[1024,2,1024]{2,0,1:T(8,128)(2,1)} async-done(((bf16[512,2,1024]{2,0,1:T(8,128)(2,1)}), bf16[1024,2,1024]{2,0,1:T(8,128)(2,1)}) %all-gather.14.cloned.1.call-update) | async-done | bytes 4194320 | tf_op jit(solution)/shard_map/all_gather | solution.py:129
  431.4 15.3 %fusion.96 = f32[1024,2,2048]{2,0,1:T(8,128)} fusion(bf16[1024,2,1024]{2,0,1:T(8,128)(2,1)} %all-gather.14.cloned.1.call-done, bf16[1024,2048]{1,0:T(8,128)(2,1)} %all-gather.16.cloned.1.call-done), kind=kOutput, calls=%fused_computation.123 | convolution fusion | flops 8589934592 | bytes 25165824 | tf_op jit(solution)/shard_map/tgd,df->tgf/dot_general | solution.py:130
  446.7 37.7 %all-gather.18.cloned.1.call-done = bf16[2048,1024]{0,1:T(8,128)(2,1)} async-done(((bf16[2048,64]{0,1:T(8,128)(2,1)}), bf16[2048,1024]{0,1:T(8,128)(2,1)}) %all-gather.18.cloned.1.call-update) | async-done | bytes 4194320 | tf_op jit(solution)/shard_map/all_gather | solution.py:96
  484.4 22.4 %fusion.58 = bf16[1024,2,2048]{2,0,1:T(8,128)(2,1)S(1)} fusion(f32[1024,2,2048]{2,0,1:T(8,128)} %fusion.96, bf16[1024,2,1024]{2,0,1:T(8,128)(2,1)} %fusion.86, bf16[2048,1024]{0,1:T(8,128)(2,1)} %all-gather.18.cloned.1.call-done), kind=kOutput, calls=%fused_computation.68 | convolution fusion | flops 8673820672 | bytes 33554432 | tf_op jit(solution)/shard_map/tgd,fd->tgf/dot_general | solution.py:144
  520.6 52.9 %reduce-scatter.12.cloned.1.call-done = bf16[512,2,1024]{2,0,1:T(8,128)(2,1)} async-done(((bf16[1024,2,1024]{2,0,1:T(8,128)(2,1)}), bf16[512,2,1024]{2,0,1:T(8,128)(2,1)}) %reduce-scatter.12.cloned.1.call-update) | async-done | bytes 2097168 | tf_op jit(solution)/shard_map/reduce_scatter | solution.py:151
  581.8 15.8 %bitcast_convert_fusion = bf16[2048,1024]{0,1:T(8,128)(2,1)} fusion(bf16[1024,2,1024]{2,0,1:T(8,128)(2,1)} %fusion.86, f32[1024,2,2048]{2,0,1:T(8,128)} %fusion.96), kind=kOutput, calls=%fused_computation.74 | convolution fusion | flops 8629780480 | bytes 25165824 | tf_op jit(solution)/shard_map/tgf,tgd->fd/dot_general | solution.py:143
  611.9 26.8 %all-gather.20.cloned.1.call-done = bf16[1024,2,1024]{2,0,1:T(8,128)(2,1)} async-done(((bf16[512,2,1024]{2,0,1:T(8,128)(2,1)}), bf16[1024,2,1024]{2,0,1:T(8,128)(2,1)}) %all-gather.20.cloned.1.call-update) | async-done | bytes 4194320 | tf_op jit(solution)/shard_map/all_gather | solution.py:164
  644.6 219.7 %while.23 = (s32[]{:T(128)}, bf16[2,3,1024,8,64]{2,4,3,1,0:T(8,128)(2,1)}, bf16[2,1024,8,64]{1,3,2,0:T(8,128)(2,1)S(1)}, bf16[2,1024,8,64]{1,3,2,0:T(8,128)(2,1)...) while((s32[]{:T(128)}, ...), condition=%wide.region_15.16_spmd, body=%wide.region_13.15_spmd.sunk | while | flops 5507637248 | bytes 272861280 | solution.py:169
  645.1 16.1 %fusion.159 = f32[8,1024,1024]{1,2,0:T(8,128)} fusion(bf16[2,1024,8,64]{1,3,2,0:T(8,128)(2,1)} %get-tuple-element.288, s32[]{:T(128)S(6)} %copy.105, bf16[2,1024,8,64]{1,3,2,0:T(8,128)(2,1)S(1)} %get-tuple-element.287), kind=kOutput, calls=%fused_computation.41.clone.1 | convolution fusion | flops 1073741824 | bytes 35652608 | tf_op jit(solution)/shard_map/while/body/eval_jaxpr/qhd,khd->hqk/dot_general | solution.py:63
  661.2 16.3 %fusion.160 = bf16[1,1,1024,8,64]{2,4,3,1,0:T(8,128)(2,1)} fusion(f32[8,1024,1024]{1,2,0:T(8,128)} %fusion.159, f32[8,1024]{1,0:T(8,128)S(1)} %dynamic-slice_bitcast_fusion.2, pred[1024,1024]{0,1:T(8,128)(4,1)S(1)} %iota_compare_fusion.5, bf16[2,1024,8,64]{1,3,2,0:T(8,128)(2,1)} %get-tuple-element.290, s32[]{:T(128)S(6)} %copy.105), kind=kOutput, calls=%fused_computation.35.clone.1 | convolution fusion | flops 1107820544 | bytes 36732932 | tf_op jit(solution)/shard_map/while/body/eval_jaxpr/hqk,qhd->khd/dot_general | solution.py:67
  677.5 24.0 %multiply_reduce_fusion.3 = (f32[8,1024]{1,0:T(8,128)S(1)}, f32[8,1024,1024]{1,2,0:T(8,128)}) fusion(f32[8,1024,1024]{1,2,0:T(8,128)} %fusion.159, f32[8,1024]{1,0:T(8,128)S(1)} %dynamic-slice_bitcast_fusion.2, pred[1024,1024]{0,1:T(8,128)(4,1)S(1)} %iota_compare_fusion.5, bf16[2,1024,8,64]{1,3,2,0:T(8,128)(2,1)} %get-tuple-element.291, ...), kind=kOutput, calls=%fused_computation.23.clone.1 | convolution fusion | flops 1115676672 | bytes 70321152 | tf_op jit(solution)/shard_map/while/body/eval_jaxpr/qhd,khd->hqk/dot_general | solution.py:70
  701.5 29.0 %multiply_convert_fusion.7 = bf16[8,1024,1024]{1,2,0:T(8,128)(2,1)} fusion(f32[8,1024,1024]{1,2,0:T(8,128)} %get-tuple-element.246, f32[8,1024,1024]{1,2,0:T(8,128)} %fusion.159, f32[8,1024]{1,0:T(8,128)S(1)} %get-tuple-element.247, f32[8,1024]{1,0:T(8,128)S(1)} %dynamic-slice_bitcast_fusion.2, pred[1024,1024]{0,1:T(8,128)(4,1)S(1)} %iota_compare_fusion.5), kind=kLoop, calls=%fused_computation.22.clone.1 | loop fusion | flops 50331648 | bytes 85000192 | tf_op jit(solution)/shard_map/while/body/eval_jaxpr/convert_element_type | solution.py:74
  756.4 14.6 %fusion.159 = f32[8,1024,1024]{1,2,0:T(8,128)} fusion(bf16[2,1024,8,64]{1,3,2,0:T(8,128)(2,1)} %get-tuple-element.288, s32[]{:T(128)S(6)} %copy.105, bf16[2,1024,8,64]{1,3,2,0:T(8,128)(2,1)S(1)} %get-tuple-element.287), kind=kOutput, calls=%fused_computation.41.clone.1 | convolution fusion | flops 1073741824 | bytes 35652608 | tf_op jit(solution)/shard_map/while/body/eval_jaxpr/qhd,khd->hqk/dot_general | solution.py:63
  771.0 16.2 %fusion.160 = bf16[1,1,1024,8,64]{2,4,3,1,0:T(8,128)(2,1)} fusion(f32[8,1024,1024]{1,2,0:T(8,128)} %fusion.159, f32[8,1024]{1,0:T(8,128)S(1)} %dynamic-slice_bitcast_fusion.2, pred[1024,1024]{0,1:T(8,128)(4,1)S(1)} %iota_compare_fusion.5, bf16[2,1024,8,64]{1,3,2,0:T(8,128)(2,1)} %get-tuple-element.290, s32[]{:T(128)S(6)} %copy.105), kind=kOutput, calls=%fused_computation.35.clone.1 | convolution fusion | flops 1107820544 | bytes 36732932 | tf_op jit(solution)/shard_map/while/body/eval_jaxpr/hqk,qhd->khd/dot_general | solution.py:67
  787.1 23.8 %multiply_reduce_fusion.3 = (f32[8,1024]{1,0:T(8,128)S(1)}, f32[8,1024,1024]{1,2,0:T(8,128)}) fusion(f32[8,1024,1024]{1,2,0:T(8,128)} %fusion.159, f32[8,1024]{1,0:T(8,128)S(1)} %dynamic-slice_bitcast_fusion.2, pred[1024,1024]{0,1:T(8,128)(4,1)S(1)} %iota_compare_fusion.5, bf16[2,1024,8,64]{1,3,2,0:T(8,128)(2,1)} %get-tuple-element.291, ...), kind=kOutput, calls=%fused_computation.23.clone.1 | convolution fusion | flops 1115676672 | bytes 70321152 | tf_op jit(solution)/shard_map/while/body/eval_jaxpr/qhd,khd->hqk/dot_general | solution.py:70
  810.9 28.5 %multiply_convert_fusion.7 = bf16[8,1024,1024]{1,2,0:T(8,128)(2,1)} fusion(f32[8,1024,1024]{1,2,0:T(8,128)} %get-tuple-element.246, f32[8,1024,1024]{1,2,0:T(8,128)} %fusion.159, f32[8,1024]{1,0:T(8,128)S(1)} %get-tuple-element.247, f32[8,1024]{1,0:T(8,128)S(1)} %dynamic-slice_bitcast_fusion.2, pred[1024,1024]{0,1:T(8,128)(4,1)S(1)} %iota_compare_fusion.5), kind=kLoop, calls=%fused_computation.22.clone.1 | loop fusion | flops 50331648 | bytes 85000192 | tf_op jit(solution)/shard_map/while/body/eval_jaxpr/convert_element_type | solution.py:74
  897.9 16.8 %fusion.107 = bf16[1024,2,1024]{2,0,1:T(8,128)(2,1)} fusion(bf16[2048,1024]{0,1:T(8,128)(2,1)} %all-gather.18.cloned.1.call-done, f32[1024,2,2048]{2,0,1:T(8,128)} %fusion.96), kind=kOutput, calls=%fused_computation.135 | convolution fusion | flops 8629780480 | bytes 25165824 | tf_op jit(solution)/shard_map/tgf,fd->tgd/dot_general | solution.py:134
  921.2 70.4 %all-reduce.14.cloned.1.call-done = bf16[3,1024,512]{2,0,1:T(4,128)(2,1)} async-done(((bf16[3,1024,512]{2,0,1:T(4,128)(2,1)}), bf16[3,1024,512]{2,0,1:T(4,128)(2,1)}) %all-reduce.14.cloned.1.call-update) | async-done | bytes 3145744
  993.5 59.1 %reduce-scatter.16.cloned.1.call-done = bf16[512,64]{0,1:T(8,128)(2,1)} async-done(((bf16[512,1024]{0,1:T(8,128)(2,1)}), bf16[512,64]{0,1:T(8,128)(2,1)}) %reduce-scatter.16.cloned.1.call-update) | async-done | bytes 65552 | tf_op jit(solution)/shard_map/reduce_scatter | solution.py:206
  1054.1 54.0 %reduce-scatter.14.cloned.1.call-done = bf16[512,2,1024]{2,0,1:T(8,128)(2,1)} async-done(((bf16[1024,2,1024]{2,0,1:T(8,128)(2,1)}), bf16[512,2,1024]{2,0,1:T(8,128)(2,1)}) %reduce-scatter.14.cloned.1.call-update) | async-done | bytes 2097168 | tf_op jit(solution)/shard_map/reduce_scatter | solution.py:184
  1113.6 33.8 %all-reduce.10 = (bf16[1024]{0:T(1024)(128)(2,1)S(1)}, bf16[1024]{0:T(1024)(128)(2,1)S(1)}, bf16[1024]{0:T(1024)(128)(2,1)S(1)}, bf16[1024]{0:T(1024)(128)(2,1)S(1)}) all-reduce(bf16[1024]{0:T(1024)(128)(2,1)S(1)} %get-tuple-element.105, bf16[1024]{0:T(1024)(128)(2,1)S(1)} %reduce_sum.141, ...), channel_id=6, replica_groups=mesh['dp'=16,'tensor'=2] {'dp'}, use_global_device_ids=true, to_apply=%region_20.21.clone | all-reduce | flops 4096 | bytes 16384
  1147.8 16.9 %reduce-scatter.10.cloned.1.call-done = bf16[512,2,1024]{2,0,1:T(8,128)(2,1)} async-done(((bf16[1024,2,1024]{2,0,1:T(8,128)(2,1)}), bf16[512,2,1024]{2,0,1:T(8,128)(2,1)}) %reduce-scatter.10.cloned.1.call-update) | async-done | bytes 2097168 | tf_op jit(solution)/shard_map/reduce_scatter | solution.py:133
  (178 shorter events, 242.9 us)
Async XLA Ops:
  7.2 46.8 %copy-start = (bf16[512,2,1024]{2,1,0:T(2,128)(2,1)S(1)}, bf16[512,2,1024]{2,1,0:T(2,128)(2,1)}, u32[]{:S(2)}) copy-start(bf16[512,2,1024]{2,1,0:T(2,128)(2,1)} %param.14) | copy-start | bytes 6291460
  7.2 103.1 %all-gather.8.cloned.1.call-start = ((), (), s32[]{:S(2)}) async-start(), calls=%async_computation.7 | async-start | bytes 6291456 | tf_op jit(solution)/shard_map/all_gather | solution.py:106
  56.2 101.6 %all-gather.10.cloned.1.call-start = ((), (), s32[]{:S(2)}) async-start(), calls=%async_computation.8 | async-start | bytes 3342336 | tf_op jit(solution)/shard_map/all_gather | solution.py:91
  56.9 203.9 %all-gather.12.cloned.1.call-start = ((), (), s32[]{:S(2)}) async-start(), calls=%async_computation.9 | async-start | bytes 1114112 | tf_op jit(solution)/shard_map/all_gather | solution.py:92
  57.6 264.0 %reduce-scatter.8.cloned.1.call-start = ((), (), s32[]{:S(2)}) async-start(), calls=%async_computation.10 | async-start | bytes 6291456 | tf_op jit(solution)/shard_map/reduce_scatter | solution.py:117
  268.4 53.3 %copy-start.1 = (bf16[512,2,1024]{2,1,0:T(2,128)(2,1)S(1)}, bf16[512,2,1024]{2,1,0:T(2,128)(2,1)}, u32[]{:S(2)}) copy-start(bf16[512,2,1024]{2,1,0:T(2,128)(2,1)} %param.14) | copy-start | bytes 6291460
  268.4 119.1 %all-gather.16.cloned.1.call-start = ((), (), s32[]{:S(2)}) async-start(), calls=%async_computation.12 | async-start | bytes 4456448 | tf_op jit(solution)/shard_map/all_gather | solution.py:95
  269.0 162.4 %all-gather.14.cloned.1.call-start = ((), (), s32[]{:S(2)}) async-start(), calls=%async_computation.11 | async-start | bytes 6291456 | tf_op jit(solution)/shard_map/all_gather | solution.py:129
  269.1 309.7 %copy-start.12 = (f32[1024]{0:T(1024)}, f32[1024]{0:T(1024)S(1)}, u32[]{:S(2)}) copy-start(f32[1024]{0:T(1024)S(1)} %convert_element_type.162) | copy-start | bytes 12292
  324.1 254.7 %copy-start.10 = (f32[512,2]{0,1:T(2,128)}, f32[512,2]{0,1:T(2,128)S(1)}, u32[]{:S(2)}) copy-start(f32[512,2]{0,1:T(2,128)S(1)} %broadcast_multiply_fusion.4) | copy-start | bytes 12292
  325.1 253.7 %copy-start.14 = (f32[512,2]{0,1:T(2,128)}, f32[512,2]{0,1:T(2,128)S(1)}, u32[]{:S(2)}) copy-start(f32[512,2]{0,1:T(2,128)S(1)} %add_rsqrt_fusion) | copy-start | bytes 12292
  327.1 157.2 %all-gather.18.cloned.1.call-start = ((), (), s32[]{:S(2)}) async-start(), calls=%async_computation.13 | async-start | bytes 4456448 | tf_op jit(solution)/shard_map/all_gather | solution.py:96
  327.9 245.6 %reduce-scatter.12.cloned.1.call-start = ((), (), s32[]{:S(2)}) async-start(), calls=%async_computation.15 | async-start | bytes 6291456 | tf_op jit(solution)/shard_map/reduce_scatter | solution.py:151
  331.5 47.7 %collective-permute-start = (bf16[512,2,1024]{2,0,1:T(8,128)(2,1)}, bf16[512,2,1024]{2,0,1:T(8,128)(2,1)}, u32[]{:S(2)}, u32[]{:S(2)}) collective-permute-start(bf16[512,2,1024]{2,0,1:T(8,128)(2,1)} %copy.45), channel_id=1, source_target_pairs={{0,1},{1,0},{2,3},{3,2},{4,5},{5,4},{6,7},{7,6},{8,9},{9,8},{10,11... | collective-permute-start | bytes 6291464 | tf_op jit(solution)/shard_map/ppermute | solution.py:15
  520.6 118.1 %all-gather.20.cloned.1.call-start = ((), (), s32[]{:S(2)}) async-start(), calls=%async_computation.16 | async-start | bytes 6291456 | tf_op jit(solution)/shard_map/all_gather | solution.py:164
  581.8 333.8 %reduce-scatter.20.cloned.1.call-start = ((), (), s32[]{:S(2)}) async-start(), calls=%async_computation.20 | async-start | bytes 4456448 | tf_op jit(solution)/shard_map/reduce_scatter | solution.py:218
  597.7 319.7 %reduce-scatter.18.cloned.1.call-start = ((), (), s32[]{:S(2)}) async-start(), calls=%async_computation.19 | async-start | bytes 4456448 | tf_op jit(solution)/shard_map/reduce_scatter | solution.py:215
  611.8 32.8 %copy-start.4 = (bf16[2,1024,8,64]{1,3,2,0:T(8,128)(2,1)S(1)}, bf16[2,1024,8,64]{1,3,2,0:T(8,128)(2,1)}, u32[]{:S(2)}) copy-start(bf16[2,1024,8,64]{1,3,2,0:T(8,128)(2,1)} %copy-done.3) | copy-start | bytes 6291460
  611.8 379.8 %all-reduce.14.cloned.1.call-start = ((), (), s32[]{:S(2)}) async-start(), calls=%async_computation.21 | async-start | bytes 8388608
  880.2 172.4 %reduce-scatter.16.cloned.1.call-start = ((), (), s32[]{:S(2)}) async-start(), calls=%async_computation.18 | async-start | bytes 1114112 | tf_op jit(solution)/shard_map/reduce_scatter | solution.py:206
  886.6 221.5 %reduce-scatter.14.cloned.1.call-start = ((), (), s32[]{:S(2)}) async-start(), calls=%async_computation.17 | async-start | bytes 6291456 | tf_op jit(solution)/shard_map/reduce_scatter | solution.py:184
  897.9 266.8 %reduce-scatter.10.cloned.1.call-start = ((), (), s32[]{:S(2)}) async-start(), calls=%async_computation.14 | async-start | bytes 6291456 | tf_op jit(solution)/shard_map/reduce_scatter | solution.py:133
  914.7 195.3 %copy-start.2 = (bf16[512,2,1024]{2,1,0:T(2,128)(2,1)S(1)}, bf16[512,2,1024]{2,1,0:T(2,128)(2,1)}, u32[]{:S(2)}) copy-start(bf16[512,2,1024]{2,1,0:T(2,128)(2,1)} %param.14) | copy-start | bytes 6291460
  914.8 195.3 %copy-start.17 = (f32[512,2]{0,1:T(2,128)S(1)}, f32[512,2]{0,1:T(2,128)}, u32[]{:S(2)}) copy-start(f32[512,2]{0,1:T(2,128)} %copy-done.16) | copy-start | bytes 12292
  914.8 195.3 %copy-start.19 = (f32[1024]{0:T(1024)S(1)}, f32[1024]{0:T(1024)}, u32[]{:S(2)}) copy-start(f32[1024]{0:T(1024)} %copy-done.18) | copy-start | bytes 12292
  914.8 195.3 %copy-start.21 = (f32[512,2]{0,1:T(2,128)S(1)}, f32[512,2]{0,1:T(2,128)}, u32[]{:S(2)}) copy-start(f32[512,2]{0,1:T(2,128)} %copy-done.20) | copy-start | bytes 12292
  921.1 192.5 %copy-start.26 = (bf16[1024]{0:T(1024)(128)(2,1)S(1)}, bf16[1024]{0:T(1024)(128)(2,1)}, u32[]{:S(2)}) copy-start(bf16[1024]{0:T(1024)(128)(2,1)} %get-tuple-element.103) | copy-start | bytes 6148
  921.1 243.5 %copy-start.11 = (f32[512,2]{0,1:T(2,128)S(1)}, f32[512,2]{0,1:T(2,128)}, u32[]{:S(2)}) copy-start(f32[512,2]{0,1:T(2,128)} %copy-done.10) | copy-start | bytes 12292
  921.1 243.5 %copy-start.13 = (f32[1024]{0:T(1024)S(1)}, f32[1024]{0:T(1024)}, u32[]{:S(2)}) copy-start(f32[1024]{0:T(1024)} %copy-done.12) | copy-start | bytes 12292
  921.2 243.5 %copy-start.15 = (f32[512,2]{0,1:T(2,128)S(1)}, f32[512,2]{0,1:T(2,128)}, u32[]{:S(2)}) copy-start(f32[512,2]{0,1:T(2,128)} %copy-done.14) | copy-start | bytes 12292
  921.2 243.5 %copy-start.23 = (f32[512,2]{0,1:T(2,128)S(1)}, f32[512,2]{0,1:T(2,128)}, u32[]{:S(2)}) copy-start(f32[512,2]{0,1:T(2,128)} %copy-done.22) | copy-start | bytes 12292
  921.2 243.5 %copy-start.25 = (f32[512,2]{0,1:T(2,128)S(1)}, f32[512,2]{0,1:T(2,128)}, u32[]{:S(2)}) copy-start(f32[512,2]{0,1:T(2,128)} %copy-done.24) | copy-start | bytes 12292
  (18 other events, 125.7 us)
Sparse Core Ops, SparseCore 0:
  56.3 53.9 all-gather.7
  112.5 45.2 all-gather.9
  159.9 36.7 all-gather.11
  268.5 53.0 reduce-scatter.7
  323.9 50.7 all-gather.15
  376.1 55.2 all-gather.13
  433.8 50.5 all-gather.17
  520.7 52.7 reduce-scatter.11
  581.9 56.7 all-gather.19
  642.4 72.4 reduce-scatter.19
  719.2 71.6 reduce-scatter.17
  880.3 111.2 all-reduce.13
  996.3 56.2 reduce-scatter.15
  1054.7 53.3 reduce-scatter.13
  1110.3 54.2 reduce-scatter.9
